TPU v7x, 512 devices: a whole 4x8x8 slice. The times are simulated.
512 devices in a mesh: section: 32 (over y, z_lo), ctx: 16 (over z_hi, x, core).
Axes of the slice: x: 4, y: 8, z: 8 (z_hi: 2, z_lo: 4; z = z_hi * 4 + z_lo), core: 2. Of those that a mesh axis runs over, the one named last changes fastest.
Arguments:
- acts: bfloat16 [32, 2, 2048, 2048], P('section', None, 'ctx'), may hold values from -8 to 8
- out_grad: bfloat16 [32, 2048, 2048], P('section', 'ctx'), may hold values from -6 to 6
- top_grad: bfloat16 [2048, 2048], P('ctx'), may hold values from -6 to 6
- gate_logits: float32 [32, 2, 16, 2048], P('section', None, None, 'ctx'), may hold values from 0 to 12
- q_gain: float32 [32, 2048], P('section'), may hold values from 0.25 to 1.75
- k_gain: float32 [32, 2048], P('section'), may hold values from 0.25 to 1.75
- doc_lengths: int32 [32, 2, 32], P('section'), may hold values from 1 to 128, 2048 in all within a row
Outputs:
- grad_first: bfloat16 [32, 2048, 2048], P('section', 'ctx')
- grad_second: bfloat16 [32, 2048, 2048], P('section', 'ctx')
- gate_grad: float32 [32, 2, 16, 2048], P('section', None, None, 'ctx')
Inputs may be any that keep to these rules, and one draw needn't show every extreme that they name: `doc_lengths`: the 32 document lengths of each segment sum to 2048, and the longest is exactly 128.
All inputs are finite; a program needn't handle non-finite values.
Results may differ from a plain program's by a relative error of at most 0.0088.
Values may be sent and summed in bfloat16 or wider, within the bound.
A program may use at most 64 MiB of HBM per device.

v0:
```python
import math

import jax
import jax.numpy as jnp
from jax import lax
from jax.sharding import PartitionSpec as P

HEAD_DIM = 128


def carried_in(value, axis, join, neutral, backward):
    count, mine = (lax.axis_size(axis), lax.axis_index(axis))
    pieces = jax.tree.map(lambda part: lax.all_gather(part, axis), value)
    if backward:
        pieces = jax.tree.map(lambda part: part[::-1], pieces)
        mine = count - 1 - mine
    subtotal = jax.tree.map(
        lambda part, zero: jnp.full_like(part, 0) + jnp.asarray(zero, part.dtype), value, neutral
    )

    def turn(position, subtotal):
        longer = join(subtotal, jax.tree.map(lambda part: part[position], pieces))
        return jax.tree.map(lambda new, old: jnp.where(position < mine, new, old), longer, subtotal)

    return lax.fori_loop(0, count - 1, turn, subtotal)


def from_behind(array, axis, by):
    peers = lax.axis_size(axis)
    pairs = [(i, i + by) for i in range(peers) if 0 <= i + by < peers]
    return lax.ppermute(array, axis, pairs)


def doc_index(lengths, positions):
    bounds = jnp.cumsum(lengths)
    return jnp.sum((bounds[None, :] <= positions[:, None]).astype(jnp.int32), axis=1)


def by_heads(values):
    return values.reshape(values.shape[0], -1, HEAD_DIM)


def joined(earlier, later):
    return (
        jnp.maximum(earlier[0], later[0]),
        jnp.where(later[0] > 0, later[1], earlier[1] + later[1]),
    )


def attend(
    query_x,
    upstream,
    query_gate,
    query_doc,
    query_pos,
    key_x,
    key_gate,
    key_doc,
    key_pos,
    gain_q,
    gain_k,
    owned,
):
    factor = 1.0 / math.sqrt(HEAD_DIM)
    queries = by_heads((query_x.astype(jnp.float32) * gain_q).astype(jnp.bfloat16))
    key_rows = by_heads((key_x.astype(jnp.float32) * gain_k).astype(jnp.bfloat16))
    values = by_heads(key_x)
    grads_in = by_heads(upstream)
    allowed = (
        (query_doc[:, None] == key_doc[None, :])
        & (key_pos[None, :] <= query_pos[:, None])
        & (key_pos[None, :] >= 0)
    )
    scores = (
        jnp.einsum("qhd,khd->hqk", queries, key_rows, preferred_element_type=jnp.float32) * factor
    )
    scores = jnp.where(allowed[None], scores + query_gate[:, :, None] - key_gate[:, None, :], -1e30)
    highest = jnp.max(scores, axis=2, keepdims=True)
    log_total = highest + jnp.log(jnp.sum(jnp.exp(scores - highest), axis=2, keepdims=True))
    weights = jnp.where(allowed[None], jnp.exp(scores - log_total), 0.0)
    weights_low = weights.astype(jnp.bfloat16)
    output = jnp.einsum("hqk,khd->qhd", weights_low, values, preferred_element_type=jnp.float32)
    row_dot = jnp.transpose(jnp.sum(grads_in.astype(jnp.float32) * output, axis=2))
    dweights = jnp.einsum("qhd,khd->hqk", grads_in, values, preferred_element_type=jnp.float32)
    dscores = weights * (dweights - row_dot[:, :, None])
    dscores_low = dscores.astype(jnp.bfloat16)
    dqueries = (
        jnp.einsum("hqk,khd->qhd", dscores_low, key_rows, preferred_element_type=jnp.float32)
        * factor
    )
    dkeys = (
        jnp.einsum("hqk,qhd->khd", dscores_low, queries, preferred_element_type=jnp.float32)
        * factor
    )
    dvalues = jnp.einsum("hqk,qhd->khd", weights_low, grads_in, preferred_element_type=jnp.float32)
    row_count = query_x.shape[0]
    return (
        dqueries.reshape(row_count, -1),
        jnp.sum(dscores, axis=2),
        dkeys.reshape(owned, -1),
        dvalues.reshape(owned, -1),
        jnp.sum(dscores, axis=1),
        log_total[:, :, 0],
        row_dot,
    )


def body(acts, out_grad, top_grad, gate_logits, q_gain, k_gain, doc_lengths):
    row_count = acts.shape[2]
    heads_here = gate_logits.shape[2]
    anchor = lax.axis_index("ctx") * row_count
    local_rows = jnp.arange(row_count, dtype=jnp.int32)
    positions = anchor + local_rows
    gain_q = q_gain[0]
    gain_k = k_gain[0]
    logits = gate_logits[0]
    log_forget = -jax.nn.softplus(-logits)
    earlier_mask = local_rows[None, :] <= local_rows[:, None]
    later_mask = local_rows[None, :] >= local_rows[:, None]
    doc_ids = []
    prior_doc = []
    next_doc = []
    gate_local = []
    reset_flags = []
    tail_sums = []
    for member in range(2):
        lengths = doc_lengths[0, member]
        own_doc = doc_index(lengths, positions)
        prior = doc_index(lengths, positions[:1] - 1)[0]
        upcoming = doc_index(lengths, positions[-1:] + 1)[0]
        same_doc = own_doc[:, None] == own_doc[None, :]
        summed = jnp.dot(
            log_forget[member],
            (same_doc & earlier_mask).astype(jnp.float32).T,
            precision=lax.Precision.HIGHEST,
        )
        doc_ids.append(own_doc)
        prior_doc.append(prior)
        next_doc.append(upcoming)
        gate_local.append(summed)
        reset_flags.append(jnp.reshape((own_doc[-1] != prior).astype(jnp.float32), (1,)))
        tail_sums.append(summed[:, -1])
    carried = carried_in(
        (jnp.stack(reset_flags), jnp.stack(tail_sums)),
        "ctx",
        joined,
        (jnp.zeros((2, 1), jnp.float32), jnp.zeros((2, heads_here), jnp.float32)),
        False,
    )
    gate_sums = []
    for member in range(2):
        carry_in = jnp.where(
            (doc_ids[member] == prior_doc[member])[None, :], carried[1][member][:, None], 0.0
        )
        gate_sums.append(gate_local[member] + carry_in)
    windows = []
    for member in range(2):
        inputs = acts[0, member]
        moved_rows = from_behind(inputs, "ctx", 1)
        moved_gates = from_behind(gate_sums[member], "ctx", 1)
        key_x = jnp.concatenate([moved_rows, inputs], axis=0)
        key_gate = jnp.concatenate([moved_gates, gate_sums[member]], axis=1)
        windows.append((key_x, key_gate))

    def member_backward(member, upstream):
        key_x, key_gate = windows[member]
        lengths = doc_lengths[0, member]
        inputs = acts[0, member]
        own_doc = doc_ids[member]
        key_pos = anchor + jnp.arange(-row_count, row_count, dtype=jnp.int32)
        key_doc = doc_index(lengths, key_pos)
        dqueries, row_sums, dkeys, dvalues, col_sums, log_total, row_dot = attend(
            inputs,
            upstream,
            gate_sums[member],
            own_doc,
            positions,
            key_x,
            key_gate,
            key_doc,
            key_pos,
            gain_q,
            gain_k,
            2 * row_count,
        )
        returned = from_behind(
            (dkeys[:row_count], dvalues[:row_count], col_sums[:, :row_count]), "ctx", -1
        )
        own_keys = dkeys[row_count:] + returned[0]
        own_values = dvalues[row_count:] + returned[1]
        own_cols = col_sums[:, row_count:] + returned[2]
        grad_inputs = (
            upstream.astype(jnp.float32) + gain_q * dqueries + gain_k * own_keys + own_values
        ).astype(jnp.bfloat16)
        gate_delta = row_sums - own_cols
        same_doc = own_doc[:, None] == own_doc[None, :]
        suffix = jnp.dot(
            gate_delta,
            (same_doc & later_mask).astype(jnp.float32).T,
            precision=lax.Precision.HIGHEST,
        )
        opens = own_doc[0] != prior_doc[member]
        reset_flag = jnp.reshape((opens | (own_doc[0] != own_doc[-1])).astype(jnp.float32), (1,))
        head_total = jnp.where(opens, 0.0, suffix[:, 0])
        carry_back = carried_in(
            (reset_flag, head_total),
            "ctx",
            joined,
            (jnp.zeros((1,), jnp.float32), jnp.zeros((heads_here,), jnp.float32)),
            True,
        )
        forget_grad = suffix + jnp.where(
            (own_doc == next_doc[member])[None, :], carry_back[1][:, None], 0.0
        )
        return (grad_inputs, forget_grad * jax.nn.sigmoid(-logits[member]))

    grad_first, gate_first = member_backward(0, out_grad[0])
    received = from_behind(grad_first, "section", -1)
    is_last = lax.axis_index("section") == lax.axis_size("section") - 1
    upstream_second = jnp.where(is_last, top_grad, received)
    grad_second, gate_second = member_backward(1, upstream_second)
    return (grad_first[None], grad_second[None], jnp.stack([gate_first, gate_second], axis=0)[None])


def solution(mesh):
    in_specs = (
        P("section", None, "ctx", None),
        P("section", "ctx", None),
        P("ctx", None),
        P("section", None, None, "ctx"),
        P("section", None),
        P("section", None),
        P("section", None, None),
    )
    out_specs = (
        P("section", "ctx", None),
        P("section", "ctx", None),
        P("section", None, None, "ctx"),
    )
    return jax.shard_map(body, mesh=mesh, in_specs=in_specs, out_specs=out_specs, check_vma=False)
```

profile of v0, /device:TPU:344, one launch (start us, length us, event | category | flops | bytes accessed | tf_op | source)
XLA Modules:
  0.0 341.4 jit_solution(3730874315594918707)
XLA Ops:
  6.8 1.3 dynamic-slice
  11.4 42.8 %all-reduce = f32[32]{0:T(128)S(1)} all-reduce(f32[32]{0:T(128)S(1)} %bitcast_dynamic-update-slice_fusion), channel_id=2, replica_groups=mesh['section'=32,'ctx'=16] {'ctx'}, use_global_device_ids=true, to_apply=%add | all-reduce | flops 32 | bytes 256
  54.6 23.8 %all-gather.4 = f32[16,2,16]{2,1,0:T(2,128)S(1)} all-gather(f32[1,2,16]{2,1,0:T(2,128)S(1)} %maximum_bitcast_fusion.1), channel_id=3, replica_groups=mesh['section'=32,'ctx'=16] {'ctx'}, dimensions={0}, use_global_device_ids=true | all-gather | bytes 2176 | tf_op jit(solution)/shard_map/all_gather | solution.py:13
  78.4 1.3 while.42
  79.7 1.2 broadcast_compare_fusion.2
  81.0 2.3 collective-permute-start.1
  83.4 1.3 fusion.60
  84.9 3.7 %collective-permute-start = (bf16[128,2048]{0,1:T(8,128)(2,1)S(1)}, bf16[128,2048]{0,1:T(8,128)(2,1)S(1)}, u32[]{:S(2)}, u32[]{:S(2)}) collective-permute-start(bf16[128,2048]{0,1:T(8,128)(2,1)S(1)} %bitcast.154), channel_id=1, source_target_pairs={{0,1},{1,2},{2,3},{3,4},{4,5},{5,6},{6,7},{7,8},{8,9},{9,10},{10,1... | collective-permute-start | bytes 1572872 | tf_op jit(solution)/shard_map/ppermute | solution.py:31
  88.9 2.2 collective-permute-start.5
  91.4 1.2 broadcast_compare_fusion.1
  94.7 18.0 %collective-permute-done = bf16[128,2048]{0,1:T(8,128)(2,1)S(1)} collective-permute-done((bf16[128,2048]{0,1:T(8,128)(2,1)S(1)}, bf16[128,2048]{0,1:T(8,128)(2,1)S(1)}, u32[]{:S(2)}, u32[]{:S(2)}) %collective-permute-start) | collective-permute-done | bytes 524320 | tf_op jit(solution)/shard_map/ppermute | solution.py:31
  113.7 2.7 fusion.64
  119.4 1.6 fusion.59
  121.0 2.6 copy.109
  123.6 1.9 collective-permute-start.3
  125.5 2.6 fusion.52
  128.7 1.2 fusion.58
  129.9 2.6 copy.107
  132.6 1.9 collective-permute-start.2
  134.6 2.4 collective-permute-start.6
  145.5 1.3 copy.110
  146.9 1.3 copy.108
  148.2 1.5 convolution_multiply_fusion.1
  149.7 1.4 copy.106
  151.1 2.1 copy.112
  153.2 8.6 %collective-permute-start.9 = (f32[16,128]{1,0:T(8,128)S(1)}, f32[16,128]{1,0:T(8,128)S(1)}, u32[]{:S(2)}, u32[]{:S(2)}) collective-permute-start(f32[16,128]{1,0:T(8,128)S(1)} %slice.185), channel_id=1, source_target_pairs={{1,0},{2,1},{3,2},{4,3},{5,4},{6,5},{7,6},{8,7},{9,8},{10,9},{11,1... | collective-permute-start | bytes 24584 | tf_op jit(solution)/shard_map/ppermute | solution.py:31
  161.8 2.8 fusion.65
  166.1 2.9 fusion.7
  169.1 1.9 collective-permute-start.4
  171.6 10.8 %collective-permute-done.4 = bf16[128,2048]{1,0:T(8,128)(2,1)} collective-permute-done((bf16[128,2048]{1,0:T(8,128)(2,1)}, bf16[128,2048]{1,0:T(8,128)(2,1)}, u32[]{:S(2)}, u32[]{:S(2)}) %collective-permute-start.4) | collective-permute-done | bytes 524320 | tf_op jit(solution)/shard_map/ppermute | solution.py:31
  184.6 1.7 convolution_bitcast_fusion.1
  187.2 1.4 fusion.53
  189.1 1.5 convolution_multiply_fusion
  190.6 1.6 fusion.57
  192.2 2.5 copy.123
  194.7 2.5 copy.122
  197.3 14.5 %collective-permute-start.8 = (f32[128,2048]{1,0:T(8,128)}, f32[128,2048]{1,0:T(8,128)}, u32[]{:S(2)}, u32[]{:S(2)}) collective-permute-start(f32[128,2048]{1,0:T(8,128)} %copy.122), channel_id=1, source_target_pairs={{1,0},{2,1},{3,2},{4,3},{5,4},{6,5},{7,6},{8,7},{9,8},{10,9},{11,1... | collective-permute-start | bytes 3145736 | tf_op jit(solution)/shard_map/ppermute | solution.py:31
  211.8 1.9 collective-permute-start.10
  213.8 1.6 fusion.56
  215.4 1.6 copy.121
  217.0 2.7 copy.120
  219.7 1.9 collective-permute-start.7
  221.6 2.5 copy.119
  224.1 23.0 %collective-permute-done.10 = f32[16,128]{1,0:T(8,128)S(1)} collective-permute-done((f32[16,128]{1,0:T(8,128)S(1)}, f32[16,128]{1,0:T(8,128)S(1)}, u32[]{:S(2)}, u32[]{:S(2)}) %collective-permute-start.10) | collective-permute-done | bytes 8224 | tf_op jit(solution)/shard_map/ppermute | solution.py:31
  247.8 51.2 %all-reduce.5 = (f32[16]{0:T(128)S(1)}, f32[256]{0:T(256)S(1)}, f32[16]{0:T(128)S(1)}, f32[256]{0:T(256)S(1)}) all-reduce(f32[16]{0:T(128)S(1)} %dynamic-update-slice.3, f32[256]{0:T(256)S(1)} %dynamic-update-slice.4, f32[16]{0:T(128)S(1)} %dynamic-update-slice.1, ...), channel_id=1, replica_groups=mesh['section'=32,'ctx'=16] {'ctx'}, use_global_device_ids=true, to_apply=%add.3 | all-reduce | flops 544 | bytes 4352
  299.1 19.1 %while.43 = (s32[]{:T(128)}, f32[16]{0:T(128)S(1)}, s32[]{:T(128)}, f32[16,1]{0,1:T(1,128)S(1)}, f32[16,16]{1,0:T(8,128)S(1)}, /*index=5*/s32[]{:T(128)}, s32[]{:T(128)}) while((s32[]{:T(128)}, f32[16]{0:T(128)S(1)}, s32[]{:T(128)}, f32[16,1]{0,1:T(1,128)S(1)}, f32[16,16]{1,0:T(8,128)S(1)}, /*index=5*/s32[]{:T(128)}, ...), condition=%wide.region_20.21_spmd.clone, body=%wide.region_19.20_spmd.clone.sunk | while | flops 69 | bytes 311 | solution.py:25
  318.4 19.1 %while.44 = (s32[]{:T(128)}, f32[16]{0:T(128)S(1)}, s32[]{:T(128)}, f32[16,1]{0,1:T(1,128)S(1)}, f32[16,16]{1,0:T(8,128)S(1)}, /*index=5*/s32[]{:T(128)}, s32[]{:T(128)}) while((s32[]{:T(128)}, f32[16]{0:T(128)S(1)}, s32[]{:T(128)}, f32[16,1]{0,1:T(1,128)S(1)}, f32[16,16]{1,0:T(8,128)S(1)}, /*index=5*/s32[]{:T(128)}, ...), condition=%wide.region_25.26_spmd.clone, body=%wide.region_24.25_spmd.clone.sunk | while | flops 69 | bytes 311 | solution.py:25
  338.2 3.2 fusion.10
  (207 shorter events, 62.2 us)
Async XLA Ops:
  81.0 11.7 %copy-start.5 = (bf16[1,128,2048]{2,1,0:T(8,128)(2,1)S(1)}, bf16[1,128,2048]{2,1,0:T(8,128)(2,1)}, u32[]{:S(2)}) copy-start(bf16[1,128,2048]{2,1,0:T(8,128)(2,1)} %param.14) | copy-start | bytes 1572868
  81.0 13.7 %collective-permute-start.1 = (f32[16,128]{1,0:T(8,128)S(1)}, f32[16,128]{1,0:T(8,128)S(1)}, u32[]{:S(2)}, u32[]{:S(2)}) collective-permute-start(f32[16,128]{1,0:T(8,128)S(1)} %select_add_fusion.1), channel_id=1, source_target_pairs={{0,1},{1,2},{2,3},{3,4},{4,5},{5,6},{6,7},{7,8},{8,9},{9,10},{10,1... | collective-permute-start | bytes 24584 | tf_op jit(solution)/shard_map/ppermute | solution.py:31
  84.9 27.8 %collective-permute-start = (bf16[128,2048]{0,1:T(8,128)(2,1)S(1)}, bf16[128,2048]{0,1:T(8,128)(2,1)S(1)}, u32[]{:S(2)}, u32[]{:S(2)}) collective-permute-start(bf16[128,2048]{0,1:T(8,128)(2,1)S(1)} %bitcast.154), channel_id=1, source_target_pairs={{0,1},{1,2},{2,3},{3,4},{4,5},{5,6},{6,7},{7,8},{8,9},{9,10},{10,1... | collective-permute-start | bytes 1572872 | tf_op jit(solution)/shard_map/ppermute | solution.py:31
  88.6 25.1 %copy-start.16 = (f32[1,2048]{1,0:T(1,128)S(1)}, f32[1,2048]{1,0:T(1,128)}, u32[]{:S(2)}) copy-start(f32[1,2048]{1,0:T(1,128)} %param.17) | copy-start | bytes 24580
  88.6 25.1 %copy-start.18 = (f32[1,2048]{1,0:T(1,128)S(1)}, f32[1,2048]{1,0:T(1,128)}, u32[]{:S(2)}) copy-start(f32[1,2048]{1,0:T(1,128)} %param.18) | copy-start | bytes 24580
  88.9 62.2 %collective-permute-start.5 = (bf16[128,2048]{0,1:T(8,128)(2,1)S(1)}, bf16[128,2048]{0,1:T(8,128)(2,1)}, u32[]{:S(2)}, u32[]{:S(2)}) collective-permute-start(bf16[128,2048]{0,1:T(8,128)(2,1)S(1)} %bitcast.150), channel_id=1, source_target_pairs={{0,1},{1,2},{2,3},{3,4},{4,5},{5,6},{6,7},{7,8},{8,9},{9,10},{10,1... | collective-permute-start | bytes 1572872 | tf_op jit(solution)/shard_map/ppermute | solution.py:31
  116.4 1.0 copy-start.7
  117.4 1.0 copy-start.11
  117.4 1.2 copy-start.14
  123.6 41.7 %collective-permute-start.3 = (f32[128,2048]{1,0:T(8,128)}, f32[128,2048]{1,0:T(8,128)}, u32[]{:S(2)}, u32[]{:S(2)}) collective-permute-start(f32[128,2048]{1,0:T(8,128)} %copy.109), channel_id=1, source_target_pairs={{1,0},{2,1},{3,2},{4,3},{5,4},{6,5},{7,6},{8,7},{9,8},{10,9},{11,1... | collective-permute-start | bytes 3145736 | tf_op jit(solution)/shard_map/ppermute | solution.py:31
  128.2 1.8 copy-start.9
  129.9 15.6 %copy-start.1 = (f32[128,16,128]{0,2,1:T(8,128)S(1)}, f32[128,16,128]{0,2,1:T(8,128)}, u32[]{:S(2)}) copy-start(f32[128,16,128]{0,2,1:T(8,128)} %get-tuple-element.417) | copy-start | bytes 3145732
  132.6 32.7 %collective-permute-start.2 = (f32[128,2048]{1,0:T(8,128)}, f32[128,2048]{1,0:T(8,128)}, u32[]{:S(2)}, u32[]{:S(2)}) collective-permute-start(f32[128,2048]{1,0:T(8,128)} %copy.107), channel_id=1, source_target_pairs={{1,0},{2,1},{3,2},{4,3},{5,4},{6,5},{7,6},{8,7},{9,8},{10,9},{11,1... | collective-permute-start | bytes 3145736 | tf_op jit(solution)/shard_map/ppermute | solution.py:31
  134.6 11.0 %collective-permute-start.6 = (f32[16,128]{1,0:T(8,128)S(1)}, f32[16,128]{1,0:T(8,128)S(1)}, u32[]{:S(2)}, u32[]{:S(2)}) collective-permute-start(f32[16,128]{1,0:T(8,128)S(1)} %select_add_fusion), channel_id=1, source_target_pairs={{0,1},{1,2},{2,3},{3,4},{4,5},{5,6},{6,7},{7,8},{8,9},{9,10},{10,1... | collective-permute-start | bytes 24584 | tf_op jit(solution)/shard_map/ppermute | solution.py:31
  145.5 2.7 copy-start.12
  146.9 1.3 copy-start.10
  153.2 17.9 %collective-permute-start.9 = (f32[16,128]{1,0:T(8,128)S(1)}, f32[16,128]{1,0:T(8,128)S(1)}, u32[]{:S(2)}, u32[]{:S(2)}) collective-permute-start(f32[16,128]{1,0:T(8,128)S(1)} %slice.185), channel_id=1, source_target_pairs={{1,0},{2,1},{3,2},{4,3},{5,4},{6,5},{7,6},{8,7},{9,8},{10,9},{11,1... | collective-permute-start | bytes 24584 | tf_op jit(solution)/shard_map/ppermute | solution.py:31
  161.8 3.5 %copy-start.4 = (f32[128,2048]{1,0:T(8,128)S(1)}, f32[128,2048]{1,0:T(8,128)}, u32[]{:S(2)}) copy-start(f32[128,2048]{1,0:T(8,128)} %copy.106) | copy-start | bytes 3145732
  161.8 3.5 %copy-start.6 = (bf16[1,128,2048]{2,1,0:T(8,128)(2,1)S(1)}, bf16[1,128,2048]{2,1,0:T(8,128)(2,1)}, u32[]{:S(2)}) copy-start(bf16[1,128,2048]{2,1,0:T(8,128)(2,1)} %param.14) | copy-start | bytes 1572868
  164.6 1.2 copy-start.2
  164.6 1.5 copy-start.3
  169.1 13.4 %collective-permute-start.4 = (bf16[128,2048]{1,0:T(8,128)(2,1)}, bf16[128,2048]{1,0:T(8,128)(2,1)}, u32[]{:S(2)}, u32[]{:S(2)}) collective-permute-start(bf16[128,2048]{1,0:T(8,128)(2,1)} %fusion.7), channel_id=1, source_target_pairs={{16,0},{32,16},{48,32},{64,48},{80,64},{96,80},{112,96},{128,112},... | collective-permute-start | bytes 1572872 | tf_op jit(solution)/shard_map/ppermute | solution.py:31
  184.6 1.7 copy-start.8
  184.6 1.7 copy-start.13
  184.6 1.7 copy-start.15
  197.3 140.9 %collective-permute-start.8 = (f32[128,2048]{1,0:T(8,128)}, f32[128,2048]{1,0:T(8,128)}, u32[]{:S(2)}, u32[]{:S(2)}) collective-permute-start(f32[128,2048]{1,0:T(8,128)} %copy.122), channel_id=1, source_target_pairs={{1,0},{2,1},{3,2},{4,3},{5,4},{6,5},{7,6},{8,7},{9,8},{10,9},{11,1... | collective-permute-start | bytes 3145736 | tf_op jit(solution)/shard_map/ppermute | solution.py:31
  211.8 35.3 %collective-permute-start.10 = (f32[16,128]{1,0:T(8,128)S(1)}, f32[16,128]{1,0:T(8,128)S(1)}, u32[]{:S(2)}, u32[]{:S(2)}) collective-permute-start(f32[16,128]{1,0:T(8,128)S(1)} %slice.188), channel_id=1, source_target_pairs={{1,0},{2,1},{3,2},{4,3},{5,4},{6,5},{7,6},{8,7},{9,8},{10,9},{11,1... | collective-permute-start | bytes 24584 | tf_op jit(solution)/shard_map/ppermute | solution.py:31
  217.0 120.5 %copy-start.17 = (f32[1,2,16,128]{3,2,1,0:T(8,128)S(1)}, f32[1,2,16,128]{3,2,1,0:T(8,128)}, u32[]{:S(2)}) copy-start(f32[1,2,16,128]{3,2,1,0:T(8,128)} %param.16) | copy-start | bytes 49156
  217.0 121.2 %copy-start = (f32[128,2048]{1,0:T(8,128)S(1)}, f32[128,2048]{1,0:T(8,128)}, u32[]{:S(2)}) copy-start(f32[128,2048]{1,0:T(8,128)} %copy.123) | copy-start | bytes 3145732
  219.7 118.5 %collective-permute-start.7 = (f32[128,2048]{1,0:T(8,128)}, f32[128,2048]{1,0:T(8,128)}, u32[]{:S(2)}, u32[]{:S(2)}) collective-permute-start(f32[128,2048]{1,0:T(8,128)} %copy.120), channel_id=1, source_target_pairs={{1,0},{2,1},{3,2},{4,3},{5,4},{6,5},{7,6},{8,7},{9,8},{10,9},{11,1... | collective-permute-start | bytes 3145736 | tf_op jit(solution)/shard_map/ppermute | solution.py:31
where the time goes:
time: 343 us; the launch traced here: 341 us
  blocking collectives  118 us (34%)
  other arithmetic  53 us (15%)
  waiting for transfers between devices  52.6 us (15%)
  local copies, waits for them, and re-layouts  44.8 us (13%)
  starting transfers between devices  43.4 us (13%)
  matrix products  18.2 us (5%)
  between operations  10.9 us (3%)
    unnamed x2, blocking collectives  93.9 us
    ppermute x11, waiting for transfers between devices, from_behind(): return lax.ppermute(array, axis, pairs)  52.6 us
    ppermute x11, starting transfers between devices, from_behind(): return lax.ppermute(array, axis, pairs)  43.4 us
    all_gather x1, blocking collectives, carried_in(): pieces = jax.tree.map(lambda part: lax.all_gather(part, axis), value)  23.8 us
    select_n x45, other arithmetic, turn(): jnp.where(position < mine, new, old)  21 us
    gt x45, other arithmetic, joined(): later[0] > 0  17.7 us
    slice x4, local copies, waits for them, and re-layouts, member_backward(): dvalues[:row_count]  8.32 us
    slice x4, local copies, waits for them, and re-layouts, member_backward(): dkeys[:row_count]  8.17 us
  transfers between devices with their start and end apart: 11, of which 4 were waited for; matrix products, arithmetic and copies ran while one was open for 25% of the time, Pallas kernels for 0%

commit v1 on v0

v1 whole, which is shorter than its diff:
```python
import functools
import math

import jax
import jax.numpy as jnp
from jax import lax
from jax.experimental import pallas as pl
from jax.experimental.pallas import tpu as pltpu
from jax.sharding import PartitionSpec as P

MESH = pl.DeviceIdType.MESH
D = 128
G = 4
W = G * D
B = 1
LOG2E = math.log2(math.e)
F32 = jnp.float32
BF16 = jnp.bfloat16
NT = (((1,), (1,)), ((), ()))
NN = (((1,), (0,)), ((), ()))
TN = (((0,), (0,)), ((), ()))


def dot(a, b, dims):
    return lax.dot_general(a, b, dims, preferred_element_type=F32)


def dot_exact(a, b, dims):
    return lax.dot_general(
        a, b, dims, preferred_element_type=F32, precision=lax.Precision.HIGHEST
    )


def kernel(
    sections,
    shards,
    acts,
    out_grad,
    top_grad,
    logits_in,
    q_gain_in,
    k_gain_in,
    docs_in,
    o_first,
    o_second,
    o_gate,
    ownx,
    logits,
    q_gain,
    k_gain,
    docs,
    prevx,
    dy,
    rrecv,
    rsend,
    outs,
    gate_out,
    passing,
    prevlog,
    crecv,
    csend,
    diff,
    base,
    bias,
    x_s,
    x_r,
    r_s,
    r_r,
    d_s,
    d_r,
    f_s,
    f_r,
    l_s,
    l_r,
    c_s,
    c_r,
    y_s,
    o_s,
    in_s,
    g_s,
):
    s = lax.axis_index("section")
    c = lax.axis_index("ctx")
    rows = acts.shape[2]
    heads = logits.shape[2]
    groups = heads // G
    half_steps = groups // B
    steps = 2 * half_steps
    has_prev = c > 0
    has_next = c < shards - 1
    sends_up = s > 0
    is_last = s == sections - 1
    prev_c = lax.rem(c + shards - 1, shards)
    next_c = lax.rem(c + 1, shards)
    prev_s = lax.rem(s + sections - 1, sections)
    next_s = lax.rem(s + 1, sections)

    relayed = shards == 16 and groups == 4
    half = shards // 2
    core = c % 2
    column = (c % half) // 2
    edge_low = (c == half - 1) if relayed else False
    edge_high = (c == half) if relayed else False
    passes_on = (c < half - 2) if relayed else False
    passes_back = (c > half + 1) if relayed else False
    on_relays = [{"ctx": n} for n in range(half - 2)]
    back_relays = [{"ctx": n} for n in range(half + 2, shards)]

    def when(condition):
        return pl.when(condition) if condition is not False else (lambda f: None)

    fetches = [
        pltpu.make_async_copy(logits_in, logits, in_s.at[0]),
        pltpu.make_async_copy(docs_in, docs, in_s.at[1]),
        pltpu.make_async_copy(q_gain_in, q_gain, in_s.at[2]),
        pltpu.make_async_copy(k_gain_in, k_gain, in_s.at[3]),
        pltpu.make_async_copy(acts.at[0, 0], ownx.at[0], in_s.at[4]),
        pltpu.make_async_copy(acts.at[0, 1], ownx.at[1], in_s.at[5]),
        pltpu.make_async_copy(out_grad.at[0], dy.at[0], in_s.at[6]),
    ]
    for i in (4, 0, 1, 2, 3, 6, 5):
        fetches[i].start()

    barrier = pltpu.get_barrier_semaphore()

    def greet(other):
        pl.semaphore_signal(barrier, inc=1, device_id=other, device_id_type=MESH)

    for other in ({"ctx": prev_c}, {"ctx": next_c}, {"section": prev_s}, {"section": next_s}):
        greet(other)

    @when(edge_low)
    def _():
        for other in back_relays:
            greet(other)

    @when(edge_high)
    def _():
        for other in on_relays:
            greet(other)

    @when(passes_on)
    def _():
        greet({"ctx": half - 1})

    @when(passes_back)
    def _():
        greet({"ctx": half})

    def lanes(n):
        return pl.ds(pl.multiple_of(n * W, W), W)

    def remote(src, dst, send, recv, where):
        return pltpu.make_async_remote_copy(
            src_ref=src,
            dst_ref=dst,
            send_sem=send,
            recv_sem=recv,
            device_id=where,
            device_id_type=MESH,
        )

    t_copy = pltpu.make_async_copy(top_grad, dy.at[1], y_s)

    def each_group(f):
        def go(n, _):
            f(n)
            return 0

        lax.fori_loop(0, groups, go, 0)

    @pl.when(is_last)
    def _():
        t_copy.start()

    peers = jnp.int32(4)
    if relayed:
        peers = peers + jnp.where(edge_low, len(on_relays), 0) + jnp.where(edge_high, len(back_relays), 0)
        peers = peers + jnp.where(passes_on | passes_back, 1, 0)
    pl.semaphore_wait(barrier, peers)

    def x_copy(g, n):
        return remote(
            ownx.at[g, :, lanes(n)],
            prevx.at[g, n],
            x_s.at[g, n],
            x_r.at[g, n],
            {"ctx": next_c},
        )

    def x_far(g, n):
        return remote(
            ownx.at[g, :, lanes(n)], passing, x_s.at[g, n], f_r, {"ctx": 2 * n + g}
        )

    def x_pass():
        return remote(
            passing, prevx.at[core, column], f_s, x_r.at[core, column], {"ctx": half}
        )

    def r_copy(g, n):
        return remote(
            rsend.at[g, n], rrecv.at[g, n], r_s.at[g, n], r_r.at[g, n], {"ctx": prev_c}
        )

    def r_far(g, n):
        return remote(rsend.at[g, n], passing, r_s.at[g, n], f_r, {"ctx": half + 2 * n + g})

    def r_pass():
        return remote(
            passing, rrecv.at[core, column], f_s, r_r.at[core, column], {"ctx": half - 1}
        )

    def d_copy(n):
        return remote(
            outs.at[0, :, lanes(n)],
            dy.at[1, :, lanes(n)],
            d_s.at[n],
            d_r.at[n],
            {"section": prev_s},
        )

    def c_copy(g):
        return remote(csend.at[g], crecv.at[g], c_s.at[g], c_r.at[g], {"ctx": prev_c})

    l_copy = remote(logits.at[0], prevlog, l_s, l_r, {"ctx": next_c})

    def x_pass_in():
        x_far(0, 0).wait_recv()
        x_pass().start()

    def r_pass_in():
        r_far(0, 0).wait_recv()
        r_pass().start()

    def send_acts(g, n):
        far = edge_low & (n < groups - 1) if relayed else False

        @when(far)
        def _():
            x_far(g, n).start()

        @pl.when(has_next & jnp.logical_not(far))
        def _():
            x_copy(g, n).start()

    def send_some(g, begin, stop):
        def go(n, _):
            send_acts(g, n)
            return 0

        lax.fori_loop(begin, stop, go, 0)

    fetches[0].wait()
    fetches[4].wait()

    @pl.when(has_next)
    def _():
        l_copy.start()

    send_some(0, 0, groups // 2)

    @pl.when(jnp.logical_not(has_prev))
    def _():
        prevx[...] = jnp.zeros_like(prevx)
        prevlog[...] = jnp.zeros_like(prevlog)

    @pl.when(jnp.logical_not(has_next))
    def _():
        rrecv[...] = jnp.zeros_like(rrecv)
        crecv[...] = jnp.zeros_like(crecv)

    for i in (1, 2, 3, 6, 5):
        fetches[i].wait()

    def log_forget(x):
        return jnp.minimum(x, 0.0) - jnp.log1p(jnp.exp(-jnp.abs(x)))

    sub = lax.broadcasted_iota(jnp.int32, (rows, rows), 0)
    lane = lax.broadcasted_iota(jnp.int32, (rows, rows), 1)
    anchor = (c * rows).astype(F32)
    own_masks = []
    prev_masks = []
    n_docs = docs.shape[2]
    for g in range(2):
        d0 = lax.broadcasted_iota(jnp.int32, (n_docs, n_docs), 0)
        d1 = lax.broadcasted_iota(jnp.int32, (n_docs, n_docs), 1)
        lengths = docs[0, g : g + 1, :].astype(F32)
        bounds = jnp.sum(jnp.where(d1 <= d0, lengths, 0.0), axis=1, keepdims=True)
        pos = lax.broadcasted_iota(jnp.int32, (n_docs, rows), 1).astype(F32) + anchor
        begin = jnp.max(jnp.where(bounds <= pos, bounds, 0.0), axis=0, keepdims=True)
        key_pos = sub.astype(F32) + anchor
        own_masks.append((key_pos >= begin) & (sub <= lane))
        prev_masks.append(key_pos - float(rows) >= begin)

    @pl.when(has_prev)
    def _():
        l_copy.wait_recv()

    def make_bias(g):
        upto = (lane <= sub).astype(F32)
        after = (lane > sub).astype(F32)
        own = dot_exact(upto, log_forget(logits[0, g]), NT) * LOG2E
        before = dot_exact(after, log_forget(prevlog[g]), NT) * -LOG2E
        for h in range(heads):
            bias[g, h, :rows] = jnp.where(prev_masks[g], -before[:, h : h + 1], -1e30)
            bias[g, h, rows:] = jnp.where(own_masks[g], -own[:, h : h + 1], -1e30)

    make_bias(0)
    send_some(0, groups // 2, groups)

    @when(passes_on & (core == 0) if relayed else False)
    def _():
        x_pass_in()

    make_bias(1)
    factor = 1.0 / math.sqrt(D)

    def load(g, n, j):
        h = n * G + j
        col = pl.ds(pl.multiple_of(h * D, D), D)
        here = slice(j * D, (j + 1) * D)
        x = ownx[g, :, col]
        xp = prevx[g, n, :, here]
        up = dy[g, :, col]
        gq = q_gain[:, col]
        gk = k_gain[:, col]
        xf = x.astype(F32)
        q = (xf * gq).astype(BF16)
        qk = (q.astype(F32) * (gk * factor)).astype(BF16)
        k = jnp.concatenate(
            [(xp.astype(F32) * gk).astype(BF16), (xf * gk).astype(BF16)], axis=0
        )
        v = jnp.concatenate([xp, x], axis=0)
        return h, here, q, qk, k, v, up, gq

    def scores_of(q, k, v, up):
        zero = jnp.zeros((rows, D), BF16)
        right = jnp.concatenate(
            [jnp.concatenate([q, zero], axis=1), jnp.concatenate([zero, up], axis=1)], axis=0
        )
        both = dot(jnp.concatenate([k, v], axis=1), right, NT)
        return both[:, :rows], both[:, rows:]

    def soft(g, h, st, dpt):
        sc = st * (factor * LOG2E) + bias[g, h]
        e = jnp.exp2(sc - jnp.max(sc, axis=0, keepdims=True))
        p = e * (1.0 / jnp.sum(e, axis=0, keepdims=True))
        row_dot = jnp.sum(p * dpt, axis=0, keepdims=True)
        ds = (p * (dpt - row_dot)).astype(BF16)
        sums = jnp.sum(ds.astype(F32), axis=0, keepdims=True)
        return p.astype(BF16), ds, sums

    def compute(step):
        g = step // half_steps
        first = (step % half_steps) * B

        @pl.when(has_prev)
        def _():
            for b in range(B):
                x_copy(g, first + b).wait_recv()

        @pl.when((step == half_steps) & is_last)
        def _():
            t_copy.wait()

        @pl.when((g == 1) & jnp.logical_not(is_last))
        def _():
            for b in range(B):
                d_copy(first + b).wait_recv()

        places = [(first + b, j) for b in range(B) for j in range(G)]
        loaded = [load(g, n, j) for n, j in places]
        raw = [scores_of(q, k, v, up) for _, _, q, _, k, v, up, _ in loaded]
        soft_out = [soft(g, item[0], *both) for item, both in zip(loaded, raw)]
        ones = jnp.ones((16, rows), BF16)
        for (n, _), item, (low, ds, sums) in zip(places, loaded, soft_out):
            h, here, q, qk, k, v, up, gq = item
            t = dot(
                jnp.concatenate([ds, low], axis=1), jnp.concatenate([qk, up], axis=0), NN
            )
            ds_t = ds.T
            dq = dot(ds_t, k, NN)
            cols = dot(ones, ds_t, NN)[:1]
            rsend[g, n, :, here] = t[:rows].astype(BF16)
            base[g, n, :, here] = up.astype(F32) + (gq * factor) * dq + t[rows:]
            csend[g, pl.ds(h, 1), :] = cols[:, :rows]
            diff[g, pl.ds(h, 1), :] = sums - cols[:, rows:]

        for b in range(B):
            n = first + b
            far = edge_high & (n > 0) if relayed else False

            @when(far)
            def _():
                r_far(g, n).start()

            @pl.when(has_prev & jnp.logical_not(far))
            def _():
                r_copy(g, n).start()

        @pl.when(has_prev & (first == groups - B))
        def _():
            c_copy(g).start()

    def finish(step):
        g = step // half_steps
        first = (step % half_steps) * B
        for b in range(B):
            n = first + b

            @pl.when(has_next)
            def _():
                r_copy(g, n).wait_recv()

            total = (base[g, n] + rrecv[g, n].astype(F32)).astype(BF16)
            outs[g, :, lanes(n)] = total

            @pl.when((g == 0) & sends_up)
            def _():
                d_copy(n).start()

            @pl.when(g == 0)
            def _():
                o_copy(0, n).start()

            @pl.when(g == 1)
            def _():
                o_copy(1, n).start()

    def o_copy(g, n):
        to = (o_first, o_second)[g]
        return pltpu.make_async_copy(outs.at[g, :, lanes(n)], to.at[0, :, lanes(n)], o_s.at[g, n])

    lag = 1 + jnp.where(edge_low, 2, 0) if relayed else 1

    def one(step, _):
        compute(step)

        @pl.when((step < half_steps) & jnp.logical_not(edge_low))
        def _():
            for b in range(B):
                send_acts(1, step * B + b)

        @when(edge_low & (step == 0) if relayed else False)
        def _():
            send_some(1, 0, groups)

        @when(passes_on & (core == 1) & (step == 1) if relayed else False)
        def _():
            x_pass_in()

        @when(passes_back & (core == 0) & (step == column + 2) if relayed else False)
        def _():
            r_pass_in()

        @pl.when(step >= lag)
        def _():
            finish(step - lag)

        return 0

    lax.fori_loop(0, steps, one, 0)

    @when(passes_back & (core == 1) if relayed else False)
    def _():
        r_pass_in()

    def gates(g):
        @pl.when(has_next)
        def _():
            c_copy(g).wait_recv()

        mask = own_masks[g].astype(F32)
        strict = jnp.where(sub < lane, mask, 0.0)
        forget = dot_exact(diff[g], mask, NT) + dot_exact(crecv[g], strict, NN)
        gate_out[0, g] = forget * jax.nn.sigmoid(-logits[0, g])

    gates(0)

    def end(step, _):
        finish(step)
        return 0

    lax.fori_loop(steps - lag, steps, end, 0)
    gates(1)
    put_gates = pltpu.make_async_copy(gate_out, o_gate, g_s)
    put_gates.start()

    @pl.when(has_next)
    def _():
        l_copy.wait_send()

        def go(n):
            x_copy(0, n).wait_send()
            x_copy(1, n).wait_send()

        each_group(go)

    @pl.when(has_prev)
    def _():
        c_copy(0).wait_send()
        c_copy(1).wait_send()

        def go(n):
            r_copy(0, n).wait_send()
            r_copy(1, n).wait_send()

        each_group(go)

    @when(passes_on)
    def _():
        x_pass().wait_send()

    @when(passes_back)
    def _():
        r_pass().wait_send()

    @pl.when(sends_up)
    def _():
        each_group(lambda n: d_copy(n).wait_send())

    def put(n):
        o_copy(0, n).wait()
        o_copy(1, n).wait()

    each_group(put)
    put_gates.wait()


def copy_out(a, b, c, out_a, out_b, out_c, held_a, held_b, held_c, got, put):
    moves = []
    for i, (src, held, dst) in enumerate(
        ((a, held_a, out_a), (b, held_b, out_b), (c, held_c, out_c))
    ):
        moves.append(
            (
                pltpu.make_async_copy(src, held, got.at[i]),
                pltpu.make_async_copy(held, dst, put.at[i]),
            )
        )
    for into, _ in moves:
        into.start()
    for into, out in moves:
        into.wait()
        out.start()
    for _, out in moves:
        out.wait()


def body(sections, shards, acts, out_grad, top_grad, logits, q_gain, k_gain, docs):
    rows = acts.shape[2]
    heads = logits.shape[2]
    groups = heads // G
    anywhere = pl.BlockSpec(memory_space=pl.ANY)
    sem = pltpu.SemaphoreType.DMA
    vmem = pltpu.VMEM
    shapes = (
        jax.ShapeDtypeStruct(out_grad.shape, BF16),
        jax.ShapeDtypeStruct(out_grad.shape, BF16),
        jax.ShapeDtypeStruct(logits.shape, F32),
    )
    results = pl.pallas_call(
        functools.partial(kernel, sections, shards),
        out_shape=shapes,
        in_specs=[anywhere] * 7,
        out_specs=(anywhere,) * 3,
        scratch_shapes=[
            vmem(acts.shape[1:], BF16),
            vmem(logits.shape, F32),
            vmem(q_gain.shape, F32),
            vmem(k_gain.shape, F32),
            vmem(docs.shape, jnp.int32),
            vmem((2, groups, rows, W), BF16),
            vmem(acts.shape[1:], BF16),
            vmem((2, groups, rows, W), BF16),
            vmem((2, groups, rows, W), BF16),
            vmem(acts.shape[1:], BF16),
            vmem(logits.shape, F32),
            vmem((rows, W), BF16),
            vmem((2, heads, rows), F32),
            vmem((2, heads, rows), F32),
            vmem((2, heads, rows), F32),
            vmem((2, heads, rows), F32),
            vmem((2, groups, rows, W), F32),
            vmem((2, heads, 2 * rows, rows), F32),
            sem((2, groups)),
            sem((2, groups)),
            sem((2, groups)),
            sem((2, groups)),
            sem((groups,)),
            sem((groups,)),
            sem,
            sem,
            sem,
            sem,
            sem((2,)),
            sem((2,)),
            sem,
            sem((2, groups)),
            sem((7,)),
            sem,
        ],
        compiler_params=pltpu.CompilerParams(
            collective_id=0, has_side_effects=True, vmem_limit_bytes=60 * 1024 * 1024
        ),
    )(acts, out_grad, top_grad, logits, q_gain, k_gain, docs)
    return pl.pallas_call(
        copy_out,
        out_shape=shapes,
        in_specs=[anywhere] * 3,
        out_specs=(anywhere,) * 3,
        scratch_shapes=[vmem(shape.shape, shape.dtype) for shape in shapes]
        + [sem((3,)), sem((3,))],
        compiler_params=pltpu.CompilerParams(vmem_limit_bytes=60 * 1024 * 1024),
    )(*results)


def solution(mesh):
    in_specs = (
        P("section", None, "ctx", None),
        P("section", "ctx", None),
        P("ctx", None),
        P("section", None, None, "ctx"),
        P("section", None),
        P("section", None),
        P("section", None, None),
    )
    out_specs = (
        P("section", "ctx", None),
        P("section", "ctx", None),
        P("section", None, None, "ctx"),
    )
    return jax.shard_map(
        functools.partial(body, mesh.shape["section"], mesh.shape["ctx"]),
        mesh=mesh,
        in_specs=in_specs,
        out_specs=out_specs,
        check_vma=False,
    )
```

time: 343 us -> 65.2 us (0.19)
  the two profiles are of different devices: /device:TPU:344 before, /device:TPU:158 now
where the time goes in v1:
time: 65.2 us; the launch traced here: 65 us
  Pallas kernels  64.4 us (99%)
    pallas_call x1, Pallas kernels, body(): pl.pallas_call(functools.partial(kernel, sections, shards), out_shape=sha...  62.3 us
    pallas_call x1, Pallas kernels, body(): pl.pallas_call(copy_out, out_shape=shapes, in_specs=[anywhere] * 3, out_s...  2.06 us

profile of v1, /device:TPU:158, one launch (start us, length us, event | category | flops | bytes accessed | tf_op | source)
XLA Modules:
  0.0 65.0 jit_solution(13487088996760865026)
XLA Ops:
  0.6 62.3 %shard_map.94 = (bf16[1,128,2048]{2,1,0:T(8,128)(2,1)}, bf16[1,128,2048]{2,1,0:T(8,128)(2,1)}, f32[1,2,16,128]{3,2,1,0:T(8,128)}) custom-call(bf16[1,2,128,2048]{3,2,1,0:T(8,128)(2,1)} %acts.1, bf16[1,128,2048]{2,1,0:T(8,128)(2,1)} %out_grad.1, bf16[128,2048]{1,0:T(8,128)(2,1)} %top_grad.1, f32[1,2,16,128]{3,2,1,0:T(8,128)} %logits_in.1, ...), custom_call_target="tpu_custom_call" | custom-call | tf_op jit(solution)/shard_map/pallas_call | solution.py:563
  63.0 2.1 %shard_map.95 = (bf16[1,128,2048]{2,1,0:T(8,128)(2,1)}, bf16[1,128,2048]{2,1,0:T(8,128)(2,1)}, f32[1,2,16,128]{3,2,1,0:T(8,128)}) custom-call(bf16[1,128,2048]{2,1,0:T(8,128)(2,1)} %get-tuple-element.6.a, bf16[1,128,2048]{2,1,0:T(8,128)(2,1)} %get-tuple-element.7.b, f32[1,2,16,128]{3,2,1,0:T(8,128)} %get-tuple-element.8.c), custom_call_target="tpu_custom_call" | custom-call | tf_op jit(solution)/shard_map/pallas_call | solution.py:608

commit v2 on v1

--- a/solution.py
+++ b/solution.py
@@ -291,7 +291,7 @@
         begin = jnp.max(jnp.where(bounds <= pos, bounds, 0.0), axis=0, keepdims=True)
         key_pos = sub.astype(F32) + anchor
         own_masks.append((key_pos >= begin) & (sub <= lane))
-        prev_masks.append(key_pos - float(rows) >= begin)
+        prev_masks.append((key_pos - float(rows) >= begin) & (sub > lane))
 
     @pl.when(has_prev)
     def _():
@@ -303,8 +303,11 @@
         own = dot_exact(upto, log_forget(logits[0, g]), NT) * LOG2E
         before = dot_exact(after, log_forget(prevlog[g]), NT) * -LOG2E
         for h in range(heads):
-            bias[g, h, :rows] = jnp.where(prev_masks[g], -before[:, h : h + 1], -1e30)
-            bias[g, h, rows:] = jnp.where(own_masks[g], -own[:, h : h + 1], -1e30)
+            bias[g, h] = jnp.where(
+                own_masks[g],
+                -own[:, h : h + 1],
+                jnp.where(prev_masks[g], -before[:, h : h + 1], -1e30),
+            )
 
     make_bias(0)
     send_some(0, groups // 2, groups)
@@ -315,11 +318,15 @@
 
     make_bias(1)
     factor = 1.0 / math.sqrt(D)
-
-    def load(g, n, j):
-        h = n * G + j
+    upto = sub <= lane
+    own_part = upto.astype(F32).astype(BF16)
+    prev_part = (sub > lane).astype(F32).astype(BF16)
+    own_part_t = (lane <= sub).astype(F32).astype(BF16)
+    prev_part_t = (lane > sub).astype(F32).astype(BF16)
+
+    def head(g, n, h):
         col = pl.ds(pl.multiple_of(h * D, D), D)
-        here = slice(j * D, (j + 1) * D)
+        here = pl.ds(pl.multiple_of((h - n * G) * D, D), D)
         x = ownx[g, :, col]
         xp = prevx[g, n, :, here]
         up = dy[g, :, col]
@@ -327,29 +334,32 @@
         gk = k_gain[:, col]
         xf = x.astype(F32)
         q = (xf * gq).astype(BF16)
-        qk = (q.astype(F32) * (gk * factor)).astype(BF16)
         k = jnp.concatenate(
             [(xp.astype(F32) * gk).astype(BF16), (xf * gk).astype(BF16)], axis=0
         )
         v = jnp.concatenate([xp, x], axis=0)
-        return h, here, q, qk, k, v, up, gq
-
-    def scores_of(q, k, v, up):
-        zero = jnp.zeros((rows, D), BF16)
-        right = jnp.concatenate(
-            [jnp.concatenate([q, zero], axis=1), jnp.concatenate([zero, up], axis=1)], axis=0
-        )
-        both = dot(jnp.concatenate([k, v], axis=1), right, NT)
-        return both[:, :rows], both[:, rows:]
-
-    def soft(g, h, st, dpt):
+        st = dot(k, q, NT)
+        dpt = dot(v, up, NT)
+        st = jnp.where(upto, st[rows:], st[:rows])
+        dpt = jnp.where(upto, dpt[rows:], dpt[:rows])
         sc = st * (factor * LOG2E) + bias[g, h]
         e = jnp.exp2(sc - jnp.max(sc, axis=0, keepdims=True))
         p = e * (1.0 / jnp.sum(e, axis=0, keepdims=True))
         row_dot = jnp.sum(p * dpt, axis=0, keepdims=True)
         ds = (p * (dpt - row_dot)).astype(BF16)
+        low = p.astype(BF16)
         sums = jnp.sum(ds.astype(F32), axis=0, keepdims=True)
-        return p.astype(BF16), ds, sums
+        turned = ds.T
+        ds_t = jnp.concatenate([turned * prev_part_t, turned * own_part_t], axis=1)
+        dk = dot(jnp.concatenate([ds * prev_part, ds * own_part], axis=0), q, NN)
+        dv = dot(jnp.concatenate([low * prev_part, low * own_part], axis=0), up, NN)
+        dq = dot(ds_t, k, NN)
+        cols = dot(jnp.ones((16, rows), BF16), ds_t, NN)[:1]
+        t = (gk * factor) * dk + dv
+        rsend[g, n, :, here] = t[:rows].astype(BF16)
+        base[g, n, :, here] = up.astype(F32) + (gq * factor) * dq + t[rows:]
+        csend[g, pl.ds(h, 1), :] = cols[:, :rows]
+        diff[g, pl.ds(h, 1), :] = sums - cols[:, rows:]
 
     def compute(step):
         g = step // half_steps
@@ -369,23 +379,13 @@
             for b in range(B):
                 d_copy(first + b).wait_recv()
 
-        places = [(first + b, j) for b in range(B) for j in range(G)]
-        loaded = [load(g, n, j) for n, j in places]
-        raw = [scores_of(q, k, v, up) for _, _, q, _, k, v, up, _ in loaded]
-        soft_out = [soft(g, item[0], *both) for item, both in zip(loaded, raw)]
-        ones = jnp.ones((16, rows), BF16)
-        for (n, _), item, (low, ds, sums) in zip(places, loaded, soft_out):
-            h, here, q, qk, k, v, up, gq = item
-            t = dot(
-                jnp.concatenate([ds, low], axis=1), jnp.concatenate([qk, up], axis=0), NN
-            )
-            ds_t = ds.T
-            dq = dot(ds_t, k, NN)
-            cols = dot(ones, ds_t, NN)[:1]
-            rsend[g, n, :, here] = t[:rows].astype(BF16)
-            base[g, n, :, here] = up.astype(F32) + (gq * factor) * dq + t[rows:]
-            csend[g, pl.ds(h, 1), :] = cols[:, :rows]
-            diff[g, pl.ds(h, 1), :] = sums - cols[:, rows:]
+        def pair(i, _):
+            h = first * G + 2 * i
+            head(g, first, h)
+            head(g, first, h + 1)
+            return 0
+
+        lax.fori_loop(0, G // 2, pair, 0)
 
         for b in range(B):
             n = first + b
@@ -432,7 +432,11 @@
         to = (o_first, o_second)[g]
         return pltpu.make_async_copy(outs.at[g, :, lanes(n)], to.at[0, :, lanes(n)], o_s.at[g, n])
 
-    lag = 1 + jnp.where(edge_low, 2, 0) if relayed else 1
+    lag = 1
+
+    def end(step, _):
+        finish(step)
+        return 0
 
     def one(step, _):
         compute(step)
@@ -454,9 +458,13 @@
         def _():
             r_pass_in()
 
-        @pl.when(step >= lag)
+        @pl.when((step >= lag) & jnp.logical_not(edge_low & (step <= half_steps)))
         def _():
             finish(step - lag)
+
+        @when(edge_low & (step == half_steps - 1) if relayed else False)
+        def _():
+            lax.fori_loop(0, half_steps, end, 0)
 
         return 0
 
@@ -477,10 +485,6 @@
         gate_out[0, g] = forget * jax.nn.sigmoid(-logits[0, g])
 
     gates(0)
-
-    def end(step, _):
-        finish(step)
-        return 0
 
     lax.fori_loop(steps - lag, steps, end, 0)
     gates(1)
@@ -583,7 +587,7 @@
             vmem((2, heads, rows), F32),
             vmem((2, heads, rows), F32),
             vmem((2, groups, rows, W), F32),
-            vmem((2, heads, 2 * rows, rows), F32),
+            vmem((2, heads, rows, rows), F32),
             sem((2, groups)),
             sem((2, groups)),
             sem((2, groups)),

time: 65.2 us -> 60.4 us (0.926)
  the two profiles are of different devices: /device:TPU:158 before, /device:TPU:93 now
where the time goes in v2:
time: 60.4 us; the launch traced here: 60.3 us
  Pallas kernels  59.6 us (99%)
  between operations  0.64 us (1%)
    pallas_call x1, Pallas kernels, body(): pl.pallas_call(functools.partial(kernel, sections, shards), out_shape=sha...  57.6 us
    pallas_call x1, Pallas kernels, body(): pl.pallas_call(copy_out, out_shape=shapes, in_specs=[anywhere] * 3, out_s...  2.06 us

profile of v2, /device:TPU:93, one launch (start us, length us, event | category | flops | bytes accessed | tf_op | source)
XLA Modules:
  0.0 60.3 jit_solution(9645060776904286513)
XLA Ops:
  0.6 57.6 %shard_map.94 = (bf16[1,128,2048]{2,1,0:T(8,128)(2,1)}, bf16[1,128,2048]{2,1,0:T(8,128)(2,1)}, f32[1,2,16,128]{3,2,1,0:T(8,128)}) custom-call(bf16[1,2,128,2048]{3,2,1,0:T(8,128)(2,1)} %acts.1, bf16[1,128,2048]{2,1,0:T(8,128)(2,1)} %out_grad.1, bf16[128,2048]{1,0:T(8,128)(2,1)} %top_grad.1, f32[1,2,16,128]{3,2,1,0:T(8,128)} %logits_in.1, ...), custom_call_target="tpu_custom_call" | custom-call | tf_op jit(solution)/shard_map/pallas_call | solution.py:567
  58.2 2.1 %shard_map.95 = (bf16[1,128,2048]{2,1,0:T(8,128)(2,1)}, bf16[1,128,2048]{2,1,0:T(8,128)(2,1)}, f32[1,2,16,128]{3,2,1,0:T(8,128)}) custom-call(bf16[1,128,2048]{2,1,0:T(8,128)(2,1)} %get-tuple-element.6.a, bf16[1,128,2048]{2,1,0:T(8,128)(2,1)} %get-tuple-element.7.b, f32[1,2,16,128]{3,2,1,0:T(8,128)} %get-tuple-element.8.c), custom_call_target="tpu_custom_call" | custom-call | tf_op jit(solution)/shard_map/pallas_call | solution.py:612

commit v3 on v1

--- a/solution.py
+++ b/solution.py
@@ -99,6 +99,7 @@
     half = shards // 2
     core = c % 2
     column = (c % half) // 2
+    back = jnp.maximum(column - 1, 0)
     edge_low = (c == half - 1) if relayed else False
     edge_high = (c == half) if relayed else False
     passes_on = (c < half - 2) if relayed else False
@@ -204,11 +205,11 @@
         )
 
     def r_far(g, n):
-        return remote(rsend.at[g, n], passing, r_s.at[g, n], f_r, {"ctx": half + 2 * n + g})
+        return remote(rsend.at[g, n], passing, r_s.at[g, n], f_r, {"ctx": half + 2 * n + 2 + g})
 
     def r_pass():
         return remote(
-            passing, rrecv.at[core, column], f_s, r_r.at[core, column], {"ctx": half - 1}
+            passing, rrecv.at[core, back], f_s, r_r.at[core, back], {"ctx": half - 1}
         )
 
     def d_copy(n):
@@ -291,7 +292,7 @@
         begin = jnp.max(jnp.where(bounds <= pos, bounds, 0.0), axis=0, keepdims=True)
         key_pos = sub.astype(F32) + anchor
         own_masks.append((key_pos >= begin) & (sub <= lane))
-        prev_masks.append(key_pos - float(rows) >= begin)
+        prev_masks.append((key_pos - float(rows) >= begin) & (sub > lane))
 
     @pl.when(has_prev)
     def _():
@@ -303,8 +304,11 @@
         own = dot_exact(upto, log_forget(logits[0, g]), NT) * LOG2E
         before = dot_exact(after, log_forget(prevlog[g]), NT) * -LOG2E
         for h in range(heads):
-            bias[g, h, :rows] = jnp.where(prev_masks[g], -before[:, h : h + 1], -1e30)
-            bias[g, h, rows:] = jnp.where(own_masks[g], -own[:, h : h + 1], -1e30)
+            bias[g, h] = jnp.where(
+                own_masks[g],
+                -own[:, h : h + 1],
+                jnp.where(prev_masks[g], -before[:, h : h + 1], -1e30),
+            )
 
     make_bias(0)
     send_some(0, groups // 2, groups)
@@ -315,6 +319,11 @@
 
     make_bias(1)
     factor = 1.0 / math.sqrt(D)
+    upto = sub <= lane
+    own_part = upto.astype(F32).astype(BF16)
+    prev_part = (sub > lane).astype(F32).astype(BF16)
+    own_part_t = (lane <= sub).astype(F32).astype(BF16)
+    prev_part_t = (lane > sub).astype(F32).astype(BF16)
 
     def load(g, n, j):
         h = n * G + j
@@ -340,7 +349,8 @@
             [jnp.concatenate([q, zero], axis=1), jnp.concatenate([zero, up], axis=1)], axis=0
         )
         both = dot(jnp.concatenate([k, v], axis=1), right, NT)
-        return both[:, :rows], both[:, rows:]
+        st = jnp.where(upto, both[rows:, :rows], both[:rows, :rows])
+        return st, jnp.where(upto, both[rows:, rows:], both[:rows, rows:])
 
     def soft(g, h, st, dpt):
         sc = st * (factor * LOG2E) + bias[g, h]
@@ -373,23 +383,30 @@
         loaded = [load(g, n, j) for n, j in places]
         raw = [scores_of(q, k, v, up) for _, _, q, _, k, v, up, _ in loaded]
         soft_out = [soft(g, item[0], *both) for item, both in zip(loaded, raw)]
-        ones = jnp.ones((16, rows), BF16)
         for (n, _), item, (low, ds, sums) in zip(places, loaded, soft_out):
             h, here, q, qk, k, v, up, gq = item
-            t = dot(
-                jnp.concatenate([ds, low], axis=1), jnp.concatenate([qk, up], axis=0), NN
+            left = jnp.concatenate(
+                [
+                    jnp.concatenate([ds * prev_part, low * prev_part], axis=1),
+                    jnp.concatenate([ds * own_part, low * own_part], axis=1),
+                ],
+                axis=0,
             )
-            ds_t = ds.T
+            t = dot(left, jnp.concatenate([qk, up], axis=0), NN)
+            turned = ds.T
+            ds_t = jnp.concatenate([turned * prev_part_t, turned * own_part_t], axis=1)
             dq = dot(ds_t, k, NN)
-            cols = dot(ones, ds_t, NN)[:1]
+            ds_turned = turned.astype(F32)
+            all_cols = jnp.sum(ds_turned, axis=0, keepdims=True)
+            own_cols = jnp.sum(jnp.where(lane <= sub, ds_turned, 0.0), axis=0, keepdims=True)
             rsend[g, n, :, here] = t[:rows].astype(BF16)
             base[g, n, :, here] = up.astype(F32) + (gq * factor) * dq + t[rows:]
-            csend[g, pl.ds(h, 1), :] = cols[:, :rows]
-            diff[g, pl.ds(h, 1), :] = sums - cols[:, rows:]
+            csend[g, pl.ds(h, 1), :] = all_cols - own_cols
+            diff[g, pl.ds(h, 1), :] = sums - own_cols
 
         for b in range(B):
             n = first + b
-            far = edge_high & (n > 0) if relayed else False
+            far = edge_high & (n < groups - 1) if relayed else False
 
             @when(far)
             def _():
@@ -432,7 +449,10 @@
         to = (o_first, o_second)[g]
         return pltpu.make_async_copy(outs.at[g, :, lanes(n)], to.at[0, :, lanes(n)], o_s.at[g, n])
 
-    lag = 1 + jnp.where(edge_low, 2, 0) if relayed else 1
+
+    def end(step, _):
+        finish(step)
+        return 0
 
     def one(step, _):
         compute(step)
@@ -450,13 +470,19 @@
         def _():
             x_pass_in()
 
-        @when(passes_back & (core == 0) & (step == column + 2) if relayed else False)
+        @when(passes_back & (core == 0) & (step == column + 1) if relayed else False)
         def _():
             r_pass_in()
 
-        @pl.when(step >= lag)
-        def _():
-            finish(step - lag)
+        early = edge_low & (step < half_steps) if relayed else False
+
+        @pl.when((step >= 1) & (step <= half_steps) & jnp.logical_not(early))
+        def _():
+            finish(step - 1)
+
+        @when(edge_low & (step == half_steps - 1) if relayed else False)
+        def _():
+            lax.fori_loop(0, half_steps - 1, end, 0)
 
         return 0
 
@@ -478,11 +504,7 @@
 
     gates(0)
 
-    def end(step, _):
-        finish(step)
-        return 0
-
-    lax.fori_loop(steps - lag, steps, end, 0)
+    lax.fori_loop(half_steps, steps, end, 0)
     gates(1)
     put_gates = pltpu.make_async_copy(gate_out, o_gate, g_s)
     put_gates.start()
@@ -583,7 +605,7 @@
             vmem((2, heads, rows), F32),
             vmem((2, heads, rows), F32),
             vmem((2, groups, rows, W), F32),
-            vmem((2, heads, 2 * rows, rows), F32),
+            vmem((2, heads, rows, rows), F32),
             sem((2, groups)),
             sem((2, groups)),
             sem((2, groups)),

time: 65.2 us -> 61.4 us (0.942)
  the two profiles are of different devices: /device:TPU:158 before, /device:TPU:118 now
where the time goes in v3:
time: 61.4 us; the launch traced here: 61.3 us
  Pallas kernels  60.6 us (99%)
  between operations  0.64 us (1%)
    pallas_call x1, Pallas kernels, body(): pl.pallas_call(functools.partial(kernel, sections, shards), out_shape=sha...  58.6 us
    pallas_call x1, Pallas kernels, body(): pl.pallas_call(copy_out, out_shape=shapes, in_specs=[anywhere] * 3, out_s...  2.06 us

profile of v3, /device:TPU:118, one launch (start us, length us, event | category | flops | bytes accessed | tf_op | source)
XLA Modules:
  0.0 61.3 jit_solution(5844505838317634865)
XLA Ops:
  0.6 58.6 %shard_map.94 = (bf16[1,128,2048]{2,1,0:T(8,128)(2,1)}, bf16[1,128,2048]{2,1,0:T(8,128)(2,1)}, f32[1,2,16,128]{3,2,1,0:T(8,128)}) custom-call(bf16[1,2,128,2048]{3,2,1,0:T(8,128)(2,1)} %acts.1, bf16[1,128,2048]{2,1,0:T(8,128)(2,1)} %out_grad.1, bf16[128,2048]{1,0:T(8,128)(2,1)} %top_grad.1, f32[1,2,16,128]{3,2,1,0:T(8,128)} %logits_in.1, ...), custom_call_target="tpu_custom_call" | custom-call | tf_op jit(solution)/shard_map/pallas_call | solution.py:585
  59.2 2.1 %shard_map.95 = (bf16[1,128,2048]{2,1,0:T(8,128)(2,1)}, bf16[1,128,2048]{2,1,0:T(8,128)(2,1)}, f32[1,2,16,128]{3,2,1,0:T(8,128)}) custom-call(bf16[1,128,2048]{2,1,0:T(8,128)(2,1)} %get-tuple-element.6.a, bf16[1,128,2048]{2,1,0:T(8,128)(2,1)} %get-tuple-element.7.b, f32[1,2,16,128]{3,2,1,0:T(8,128)} %get-tuple-element.8.c), custom_call_target="tpu_custom_call" | custom-call | tf_op jit(solution)/shard_map/pallas_call | solution.py:630

commit v4 on v3

--- a/solution.py
+++ b/solution.py
@@ -99,7 +99,6 @@
     half = shards // 2
     core = c % 2
     column = (c % half) // 2
-    back = jnp.maximum(column - 1, 0)
     edge_low = (c == half - 1) if relayed else False
     edge_high = (c == half) if relayed else False
     passes_on = (c < half - 2) if relayed else False
@@ -205,11 +204,11 @@
         )
 
     def r_far(g, n):
-        return remote(rsend.at[g, n], passing, r_s.at[g, n], f_r, {"ctx": half + 2 * n + 2 + g})
+        return remote(rsend.at[g, n], passing, r_s.at[g, n], f_r, {"ctx": half + 2 * n + g})
 
     def r_pass():
         return remote(
-            passing, rrecv.at[core, back], f_s, r_r.at[core, back], {"ctx": half - 1}
+            passing, rrecv.at[core, column], f_s, r_r.at[core, column], {"ctx": half - 1}
         )
 
     def d_copy(n):
@@ -406,7 +405,7 @@
 
         for b in range(B):
             n = first + b
-            far = edge_high & (n < groups - 1) if relayed else False
+            far = edge_high & (n > 0) if relayed else False
 
             @when(far)
             def _():
@@ -470,11 +469,11 @@
         def _():
             x_pass_in()
 
-        @when(passes_back & (core == 0) & (step == column + 1) if relayed else False)
+        @when(passes_back & (core == 0) & (step == column + 3) if relayed else False)
         def _():
             r_pass_in()
 
-        early = edge_low & (step < half_steps) if relayed else False
+        early = edge_low & (step <= half_steps) if relayed else False
 
         @pl.when((step >= 1) & (step <= half_steps) & jnp.logical_not(early))
         def _():
@@ -482,7 +481,7 @@
 
         @when(edge_low & (step == half_steps - 1) if relayed else False)
         def _():
-            lax.fori_loop(0, half_steps - 1, end, 0)
+            lax.fori_loop(0, half_steps, end, 0)
 
         return 0
 

time: 61.4 us -> 63.9 us (1.041)
  the two profiles are of different devices: /device:TPU:118 before, /device:TPU:55 now
where the time goes in v4:
time: 63.9 us; the launch traced here: 63.7 us
  Pallas kernels  63.1 us (99%)
  between operations  0.64 us (1%)
    pallas_call x1, Pallas kernels, body(): pl.pallas_call(functools.partial(kernel, sections, shards), out_shape=sha...  61 us
    pallas_call x1, Pallas kernels, body(): pl.pallas_call(copy_out, out_shape=shapes, in_specs=[anywhere] * 3, out_s...  2.06 us

profile of v4, /device:TPU:55, one launch (start us, length us, event | category | flops | bytes accessed | tf_op | source)
XLA Modules:
  0.0 63.7 jit_solution(6274180389628252615)
XLA Ops:
  0.6 61.0 %shard_map.94 = (bf16[1,128,2048]{2,1,0:T(8,128)(2,1)}, bf16[1,128,2048]{2,1,0:T(8,128)(2,1)}, f32[1,2,16,128]{3,2,1,0:T(8,128)}) custom-call(bf16[1,2,128,2048]{3,2,1,0:T(8,128)(2,1)} %acts.1, bf16[1,128,2048]{2,1,0:T(8,128)(2,1)} %out_grad.1, bf16[128,2048]{1,0:T(8,128)(2,1)} %top_grad.1, f32[1,2,16,128]{3,2,1,0:T(8,128)} %logits_in.1, ...), custom_call_target="tpu_custom_call" | custom-call | tf_op jit(solution)/shard_map/pallas_call | solution.py:584
  61.7 2.1 %shard_map.95 = (bf16[1,128,2048]{2,1,0:T(8,128)(2,1)}, bf16[1,128,2048]{2,1,0:T(8,128)(2,1)}, f32[1,2,16,128]{3,2,1,0:T(8,128)}) custom-call(bf16[1,128,2048]{2,1,0:T(8,128)(2,1)} %get-tuple-element.6.a, bf16[1,128,2048]{2,1,0:T(8,128)(2,1)} %get-tuple-element.7.b, f32[1,2,16,128]{3,2,1,0:T(8,128)} %get-tuple-element.8.c), custom_call_target="tpu_custom_call" | custom-call | tf_op jit(solution)/shard_map/pallas_call | solution.py:629

commit v5 on v4

--- a/solution.py
+++ b/solution.py
@@ -102,9 +102,9 @@
     edge_low = (c == half - 1) if relayed else False
     edge_high = (c == half) if relayed else False
     passes_on = (c < half - 2) if relayed else False
-    passes_back = (c > half + 1) if relayed else False
+    passes_back = (c > half + 1) & (core == 0) if relayed else False
     on_relays = [{"ctx": n} for n in range(half - 2)]
-    back_relays = [{"ctx": n} for n in range(half + 2, shards)]
+    back_relays = [{"ctx": n} for n in range(half + 2, shards, 2)]
 
     def when(condition):
         return pl.when(condition) if condition is not False else (lambda f: None)
@@ -405,7 +405,7 @@
 
         for b in range(B):
             n = first + b
-            far = edge_high & (n > 0) if relayed else False
+            far = edge_high & (g == 0) & (n > 0) if relayed else False
 
             @when(far)
             def _():
@@ -469,7 +469,7 @@
         def _():
             x_pass_in()
 
-        @when(passes_back & (core == 0) & (step == column + 3) if relayed else False)
+        @when(passes_back & (step == column + 3) if relayed else False)
         def _():
             r_pass_in()
 
@@ -486,10 +486,6 @@
         return 0
 
     lax.fori_loop(0, steps, one, 0)
-
-    @when(passes_back & (core == 1) if relayed else False)
-    def _():
-        r_pass_in()
 
     def gates(g):
         @pl.when(has_next)

time: 63.9 us -> 63.1 us (0.987)
  Pallas kernels: 63.1 us -> 62.3 us
    pallas_call x1, Pallas kernels: 61 us -> 60.2 us  [body(): pl.pallas_call(functools.partial(kernel, sections, shards), out_shape=sha...]
where the time goes in v5:
time: 63.1 us; the launch traced here: 62.9 us
  Pallas kernels  62.3 us (99%)
  between operations  0.64 us (1%)
    pallas_call x1, Pallas kernels, body(): pl.pallas_call(functools.partial(kernel, sections, shards), out_shape=sha...  60.2 us
    pallas_call x1, Pallas kernels, body(): pl.pallas_call(copy_out, out_shape=shapes, in_specs=[anywhere] * 3, out_s...  2.06 us

profile of v5, /device:TPU:55, one launch (start us, length us, event | category | flops | bytes accessed | tf_op | source)
XLA Modules:
  0.0 62.9 jit_solution(4314493621232332427)
XLA Ops:
  0.6 60.2 %shard_map.94 = (bf16[1,128,2048]{2,1,0:T(8,128)(2,1)}, bf16[1,128,2048]{2,1,0:T(8,128)(2,1)}, f32[1,2,16,128]{3,2,1,0:T(8,128)}) custom-call(bf16[1,2,128,2048]{3,2,1,0:T(8,128)(2,1)} %acts.1, bf16[1,128,2048]{2,1,0:T(8,128)(2,1)} %out_grad.1, bf16[128,2048]{1,0:T(8,128)(2,1)} %top_grad.1, f32[1,2,16,128]{3,2,1,0:T(8,128)} %logits_in.1, ...), custom_call_target="tpu_custom_call" | custom-call | tf_op jit(solution)/shard_map/pallas_call | solution.py:580
  60.8 2.1 %shard_map.95 = (bf16[1,128,2048]{2,1,0:T(8,128)(2,1)}, bf16[1,128,2048]{2,1,0:T(8,128)(2,1)}, f32[1,2,16,128]{3,2,1,0:T(8,128)}) custom-call(bf16[1,128,2048]{2,1,0:T(8,128)(2,1)} %get-tuple-element.6.a, bf16[1,128,2048]{2,1,0:T(8,128)(2,1)} %get-tuple-element.7.b, f32[1,2,16,128]{3,2,1,0:T(8,128)} %get-tuple-element.8.c), custom_call_target="tpu_custom_call" | custom-call | tf_op jit(solution)/shard_map/pallas_call | solution.py:625

commit v6 on v2

--- a/solution.py
+++ b/solution.py
@@ -101,6 +101,7 @@
     column = (c % half) // 2
     edge_low = (c == half - 1) if relayed else False
     edge_high = (c == half) if relayed else False
+    before_edge = (c == half - 2) if relayed else False
     passes_on = (c < half - 2) if relayed else False
     passes_back = (c > half + 1) if relayed else False
     on_relays = [{"ctx": n} for n in range(half - 2)]
@@ -458,7 +459,9 @@
         def _():
             r_pass_in()
 
-        @pl.when((step >= lag) & jnp.logical_not(edge_low & (step <= half_steps)))
+        held = (edge_low & (step <= half_steps)) | (before_edge & (step > half_steps))
+
+        @pl.when((step >= lag) & jnp.logical_not(held))
         def _():
             finish(step - lag)
 
@@ -486,7 +489,7 @@
 
     gates(0)
 
-    lax.fori_loop(steps - lag, steps, end, 0)
+    lax.fori_loop(jnp.where(before_edge, half_steps, steps - lag), steps, end, 0)
     gates(1)
     put_gates = pltpu.make_async_copy(gate_out, o_gate, g_s)
     put_gates.start()

time: 60.4 us -> 58 us (0.960)
  the two profiles are of different devices: /device:TPU:93 before, /device:TPU:94 now
where the time goes in v6:
time: 58 us; the launch traced here: 57.8 us
  Pallas kernels  57.2 us (99%)
  between operations  0.64 us (1%)
    pallas_call x1, Pallas kernels, body(): pl.pallas_call(functools.partial(kernel, sections, shards), out_shape=sha...  55.1 us
    pallas_call x1, Pallas kernels, body(): pl.pallas_call(copy_out, out_shape=shapes, in_specs=[anywhere] * 3, out_s...  2.06 us

profile of v6, /device:TPU:94, one launch (start us, length us, event | category | flops | bytes accessed | tf_op | source)
XLA Modules:
  0.0 57.8 jit_solution(11215223135816208373)
XLA Ops:
  0.6 55.1 %shard_map.94 = (bf16[1,128,2048]{2,1,0:T(8,128)(2,1)}, bf16[1,128,2048]{2,1,0:T(8,128)(2,1)}, f32[1,2,16,128]{3,2,1,0:T(8,128)}) custom-call(bf16[1,2,128,2048]{3,2,1,0:T(8,128)(2,1)} %acts.1, bf16[1,128,2048]{2,1,0:T(8,128)(2,1)} %out_grad.1, bf16[128,2048]{1,0:T(8,128)(2,1)} %top_grad.1, f32[1,2,16,128]{3,2,1,0:T(8,128)} %logits_in.1, ...), custom_call_target="tpu_custom_call" | custom-call | tf_op jit(solution)/shard_map/pallas_call | solution.py:570
  55.8 2.1 %shard_map.95 = (bf16[1,128,2048]{2,1,0:T(8,128)(2,1)}, bf16[1,128,2048]{2,1,0:T(8,128)(2,1)}, f32[1,2,16,128]{3,2,1,0:T(8,128)}) custom-call(bf16[1,128,2048]{2,1,0:T(8,128)(2,1)} %get-tuple-element.6.a, bf16[1,128,2048]{2,1,0:T(8,128)(2,1)} %get-tuple-element.7.b, f32[1,2,16,128]{3,2,1,0:T(8,128)} %get-tuple-element.8.c), custom_call_target="tpu_custom_call" | custom-call | tf_op jit(solution)/shard_map/pallas_call | solution.py:615
